TPU v7x, 256 devices: a whole 4x4x8 slice. The times are simulated.
256 devices in a mesh: plane: 8 (over z_hi, core), ray: 32 (over x, y, z_lo).
Axes of the slice: x: 4, y: 4, z: 8 (z_hi: 4, z_lo: 2; z = z_hi * 2 + z_lo), core: 2. Of those that a mesh axis runs over, the one named last changes fastest.
Arguments:
- kappa: bfloat16 [2, 256, 16384], P(None, 'plane', 'ray'), may hold values from 0.049804688 to 2
- row_kernel: float32 [4, 63], replicated, may hold values from -0.75 to 0.75
- col_kernel: float32 [4, 63], replicated, may hold values from -0.75 to 0.75
- positions: float32 [2, 1048576], P(None, ('plane', 'ray')), may hold values from -6 to 6
- cells: int32 [2, 1048576], P(None, ('plane', 'ray')), may hold values from 0 to 131071
- owners: int32 [2, 8192, 1], P(None, ('plane', 'ray')), may hold values from 0 to 31; in each aligned block of 32 rows (0 to 31, 32 to 63, ..., all dimensions but the last counted through in order) at most 2 rows name the same one
- counts: int32 [256], P(('plane', 'ray')), may hold values from 24 to 32, as said below
Outputs:
- final_positions: float32 [2, 1048576], P(None, ('plane', 'ray'))
- jacobian: float32 [4, 1048576], P(None, ('plane', 'ray'))
Inputs may be any that keep to these rules, and one draw needn't show every extreme that they name: `owners`: in each aligned run of 32 blocks of one plane no tile is named by more than 2 blocks, a bound that some block reaches. `counts`: some group has all 32 blocks traced and some group exactly 24.
All inputs are finite; a program needn't handle non-finite values.
Results may differ from a plain program's by a relative error of at most 0.0023.
Values may be sent and summed in bfloat16 or wider, within the bound.
A program may use at most 320 MiB of HBM per device.

v0:
```python
import jax
import jax.numpy as jnp
from jax import lax
from jax.sharding import PartitionSpec as P

CAP = 2


lens_weights = (0.6, 0.4)


def with_halo(block, sides, width):
    for axis, dim in sides:
        count = lax.axis_size(axis)
        forward = [(i, i + 1) for i in range(count - 1)]
        backward = [(target, source) for source, target in forward]
        low = lax.ppermute(
            lax.slice_in_dim(block, block.shape[dim] - width, None, axis=dim), axis, forward
        )
        high = lax.ppermute(lax.slice_in_dim(block, 0, width, axis=dim), axis, backward)
        block = jnp.concatenate([low, block, high], axis=dim)
    return block


def from_behind(block, axis, distance):
    devices = range(lax.axis_size(axis))
    route = [(i - distance, i) for i in devices if i - distance in devices]
    return lax.ppermute(block, axis, route)


def advance(ray_state, samples, plane_weight):
    pos_x, pos_y, jac_xx, jac_xy, jac_yx, jac_yy = ray_state
    deflect_x, deflect_y, shear_one, shear_two, converge = samples
    mat_xx = converge + shear_one
    mat_yy = converge - shear_one
    return (
        pos_x - plane_weight * deflect_x,
        pos_y - plane_weight * deflect_y,
        jac_xx - plane_weight * (mat_xx * jac_xx + shear_two * jac_yx),
        jac_xy - plane_weight * (mat_xx * jac_xy + shear_two * jac_yy),
        jac_yx - plane_weight * (shear_two * jac_xx + mat_yy * jac_yx),
        jac_yy - plane_weight * (shear_two * jac_xy + mat_yy * jac_yy),
    )


def toeplitz(kernel, length_in, length_out):
    tap_count = kernel.shape[1]
    offset = jnp.arange(length_in)[:, None] - jnp.arange(length_out)[None, :]
    inside = (offset >= 0) & (offset < tap_count)
    picked = jnp.take(kernel, jnp.clip(offset, 0, tap_count - 1), axis=1)
    return jnp.where(inside[None], picked, 0.0)


def separable(padded, row_kernel, col_kernel):
    margin = (row_kernel.shape[1] - 1) // 2
    rows_in = padded.shape[1]
    cols_in = padded.shape[2]
    column_table = toeplitz(col_kernel, cols_in, cols_in - 2 * margin)
    row_table = toeplitz(row_kernel, rows_in, rows_in - 2 * margin)
    column_pass = jnp.einsum(
        "prq,cqj->pcrj", padded.astype(jnp.float32), column_table, precision=lax.Precision.HIGHEST
    )
    return jnp.einsum("cqi,pcqj->pcij", row_table, column_pass, precision=lax.Precision.HIGHEST)


def lookup(lookup_tile, cell_ids):
    flat_tile = lookup_tile.reshape(lookup_tile.shape[0], -1)
    return jnp.take(flat_tile, cell_ids, axis=1).astype(jnp.float32)


def trace_state(lookup_tile, plane_weight, incoming):
    lead_shape = incoming.shape[:-2]
    block_rays = incoming.shape[-1]
    flat_in = incoming.reshape(-1, 7, block_rays)
    slot_count = flat_in.shape[0]
    cell_ids = flat_in[:, 6].astype(jnp.int32).reshape(-1)
    samples = lookup(lookup_tile, cell_ids).reshape(5, slot_count, block_rays)
    ray_state = [flat_in[:, member] for member in range(6)]
    updated = advance(ray_state, [samples[member] for member in range(5)], plane_weight)
    return jnp.stack(updated, axis=1).reshape(lead_shape + (6, block_rays))


def local(kappa, row_kernel, col_kernel, positions, cells, owners, counts):
    margin = (row_kernel.shape[1] - 1) // 2
    own_rows = kappa.shape[1]
    widened = with_halo(kappa, (("ray", 2),), margin)
    hops = (margin + own_rows - 1) // own_rows
    neighbours = {}
    for step in list(range(hops, 0, -1)) + list(range(-1, -hops - 1, -1)):
        neighbours[step] = from_behind(widened, "plane", step)
    stacked = jnp.concatenate([neighbours[1]] + [widened] + [neighbours[-1]], axis=1)
    padded = stacked[:, hops * own_rows - margin : hops * own_rows + own_rows + margin]
    convolved = separable(padded, row_kernel, col_kernel)
    fields = jnp.concatenate([convolved.astype(jnp.bfloat16), kappa[:, None]], axis=1)
    tile_stack = lax.all_gather(fields, "plane", axis=2, tiled=True)
    block_count = owners.shape[1]
    block_rays = positions.shape[1] // block_count
    tile_owners = lax.axis_size("ray")
    block_ids = jnp.arange(block_count)
    traced = block_ids < counts[0]
    coords = positions.reshape(2, block_count, block_rays).transpose(1, 0, 2)
    identity = jnp.array([1.0, 0.0, 0.0, 1.0], jnp.float32)
    jacobi_init = jnp.broadcast_to(identity[None, :, None], (block_count, 4, block_rays))
    ray_state = jnp.concatenate([coords, jacobi_init], axis=1)
    cell_float = cells.reshape(2, block_count, 1, block_rays).astype(jnp.float32)
    selections = []
    for plane_id in range(2):
        targets = owners[plane_id, :, 0]
        slot_of = jnp.sum(
            (targets[:, None] == targets[None, :]) & (block_ids[:, None] > block_ids[None, :]),
            axis=1,
        )
        selections.append(
            (
                (targets[None, None, :] == jnp.arange(tile_owners)[:, None, None])
                & (slot_of[None, None, :] == jnp.arange(CAP)[None, :, None])
                & traced[None, None, :]
            ).astype(jnp.float32)
        )
    for plane_id in range(2):
        selection = selections[plane_id]
        packed = jnp.concatenate([ray_state, cell_float[plane_id]], axis=1)
        outgoing = jnp.einsum("scb,bvr->scvr", selection, packed, precision=lax.Precision.HIGHEST)

        def visit(incoming, lookup_tile=tile_stack[plane_id], plane_weight=lens_weights[plane_id]):
            updated = trace_state(lookup_tile, plane_weight, incoming)
            return lax.all_to_all(updated, "ray", split_axis=0, concat_axis=0, tiled=True)

        returned = visit(lax.all_to_all(outgoing, "ray", split_axis=0, concat_axis=0, tiled=True))
        arrived = jnp.einsum("scb,scvr->bvr", selection, returned, precision=lax.Precision.HIGHEST)
        ray_state = jnp.where(traced[:, None, None], arrived, ray_state)
    final_positions = ray_state[:, :2].transpose(1, 0, 2).reshape(2, block_count * block_rays)
    jacobian = ray_state[:, 2:].transpose(1, 0, 2).reshape(4, block_count * block_rays)
    return (final_positions, jacobian)


def solution(mesh):
    return jax.shard_map(
        local,
        mesh=mesh,
        in_specs=(
            P(None, "plane", "ray"),
            P(),
            P(),
            P(None, ("plane", "ray")),
            P(None, ("plane", "ray")),
            P(None, ("plane", "ray"), None),
            P(("plane", "ray")),
        ),
        out_specs=(P(None, ("plane", "ray")), P(None, ("plane", "ray"))),
        check_vma=False,
    )
```

profile of v0, /device:TPU:1, one launch (start us, length us, event | category | flops | bytes accessed | tf_op | source)
XLA Modules:
  0.0 1796.8 jit_solution(7598405827342885853)
XLA Ops:
  7.2 0.8 fusion.108
  8.0 1.3 collective-permute-start.1
  9.3 5.0 collective-permute-start
  14.3 0.2 compare_select_fusion
  14.5 0.3 fusion.21
  15.0 0.2 broadcast_clamp_fusion
  15.2 0.3 copy-done.18
  15.6 0.1 copy.57
  15.7 965.9 %gather_fusion = f32[293888,4]{1,0:T(8,128)} fusion(f32[4,63]{0,1:T(8,128)S(1)} %copy.57, s32[293888]{0:T(1024)S(1)} %broadcast_clamp_fusion), kind=kCustom, calls=%fused_computation.2 | custom fusion | bytes 10579968 | tf_op jit(solution)/shard_map/jit(_take)/gather | solution.py:50
  981.6 80.8 %copy.58 = f32[574,512,4]{1,0,2:T(8,128)} copy(f32[574,512,4]{2,1,0:T(8,128)} %bitcast.12) | data formatting | bytes 9404416 | tf_op jit(solution)/shard_map/jit(_take)/gather | solution.py:50
  1062.4 0.1 copy.59
  1062.5 8.2 gather_fusion.1
  1070.8 1.0 copy.60
  1071.8 0.1 pad_maximum_fusion.8
  1071.9 4.7 collective-permute-start.3
  1076.6 3.1 collective-permute-start.2
  1079.7 0.2 collective-permute-done.3
  1079.9 1.3 collective-permute-done.2
  1081.1 5.6 fusion
  1086.8 1.1 fusion.23
  1087.9 0.8 pad_maximum_fusion
  1089.4 0.1 convert_reduce_fusion
  1089.7 0.4 fusion.33
  1090.1 0.9 copy.55
  1091.0 11.4 all-to-all-start
  1102.5 7.8 all-to-all-done
  1110.5 0.6 copy-done
  1111.1 24.5 %all-gather.2.cloned.1.call-done = bf16[2,5,256,512]{3,2,0,1:T(8,128)(2,1)} async-done(((bf16[2,5,32,512]{3,2,0,1:T(8,128)(2,1)}), bf16[2,5,256,512]{3,2,0,1:T(8,128)(2,1)}) %all-gather.2.cloned.1.call-update) | async-done | bytes 2621456 | tf_op jit(solution)/shard_map/all_gather | solution.py:95
  1135.6 1.9 fusion.107
  1137.6 22.4 %copy.80 = bf16[1,5,256,512]{1,3,2,0:T(8,128)(2,1)} copy(bf16[1,5,256,512]{3,2,0,1:T(8,128)(2,1)S(1)} %get-tuple-element.14) | data formatting | bytes 2621440 | tf_op jit(solution)/shard_map/reshape;squeeze | solution.py:67
  1159.9 253.3 %gather_fusion.2 = bf16[8192,5]{1,0:T(8,128)(2,1)S(1)} fusion(bf16[5,131072]{0,1:T(8,128)(2,1)} %bitcast.223, s32[8192]{0:T(1024)S(1)} %fusion.78), kind=kCustom, calls=%fused_computation.clone | custom fusion | bytes 196608 | tf_op jit(solution)/shard_map/jit(_take)/gather | solution.py:68
  1413.2 1.4 bitcast_convert_fusion.1
  1414.7 10.3 subtract_reduce_fusion.1
  1425.2 0.7 copy.62
  1425.9 26.0 %all-to-all-start.1 = ((f32[32,2,6,128]{3,1,2,0:T(2,128)}), f32[32,2,6,128]{3,1,2,0:T(2,128)S(1)}, u32[]{:S(2)}, u32[]{:S(2)}) async-start(f32[32,2,6,128]{3,1,2,0:T(2,128)} %copy.62), calls=%async_computation.1 | async-start | bytes 393216 | tf_op jit(solution)/shard_map/all_to_all | solution.py:127
  1452.1 7.9 all-to-all-done.1
  1460.0 0.3 fusion.26
  1460.3 0.4 fusion.38
  1460.7 0.9 copy.65
  1461.6 4.1 all-to-all-start.2
  1465.7 22.4 %copy.81 = bf16[1,5,256,512]{1,3,2,0:T(8,128)(2,1)} copy(bf16[1,5,256,512]{3,2,0,1:T(8,128)(2,1)S(1)} %get-tuple-element.13) | data formatting | bytes 2621440 | tf_op jit(solution)/shard_map/reshape;squeeze | solution.py:67
  1488.2 253.3 %gather_fusion.3 = bf16[8192,5]{1,0:T(8,128)(2,1)S(1)} fusion(bf16[5,131072]{0,1:T(8,128)(2,1)} %bitcast.222, s32[8192]{0:T(1024)S(1)} %fusion.79), kind=kCustom, calls=%fused_computation.1.clone | custom fusion | bytes 196608 | tf_op jit(solution)/shard_map/jit(_take)/gather | solution.py:68
  1741.4 1.4 bitcast_convert_fusion
  1742.9 10.3 subtract_reduce_fusion
  1753.5 34.8 %all_to_all.20 = f32[32,2,6,128]{3,1,2,0:T(2,128)S(1)} all-to-all(f32[32,2,6,128]{3,1,2,0:T(2,128)S(1)} %copy.68), channel_id=1, replica_groups=mesh['plane'=8,'ray'=32] {'ray'}, dimensions={0} | all-to-all | bytes 393216 | tf_op jit(solution)/shard_map/all_to_all | solution.py:127
  1788.3 0.3 fusion.27
  1788.6 0.6 copy.93
  1789.3 0.7 copy.92
  (86 shorter events, 1.2 us)
Async XLA Ops:
  7.2 1128.4 %all-gather.2.cloned.1.call-start = ((), (), s32[]{:S(2)}) async-start(), calls=%async_computation.4 | async-start | bytes 2949120 | tf_op jit(solution)/shard_map/all_gather | solution.py:95
  8.0 1063.8 %collective-permute-start.1 = (bf16[2,32,31]{2,1,0:T(8,128)(2,1)S(1)}, bf16[2,32,31]{2,1,0:T(8,128)(2,1)S(1)}, u32[]{:S(2)}, u32[]{:S(2)}) collective-permute-start(bf16[2,32,31]{2,1,0:T(8,128)(2,1)S(1)} %get-tuple-element.32), channel_id=1, source_target_pairs={{1,0},{2,1},{3,2},{4,3},{5,4},{6,5},{7,6},{8,7},{9,8},{10,9},{11,1... | collective-permute-start | bytes 11912 | tf_op jit(solution)/shard_map/ppermute | solution.py:20
  9.3 1062.5 %collective-permute-start = (bf16[2,32,31]{2,1,0:T(8,128)(2,1)S(1)}, bf16[2,32,31]{2,1,0:T(8,128)(2,1)S(1)}, u32[]{:S(2)}, u32[]{:S(2)}) collective-permute-start(bf16[2,32,31]{2,1,0:T(8,128)(2,1)S(1)} %get-tuple-element.31), channel_id=1, source_target_pairs={{0,1},{1,2},{2,3},{3,4},{4,5},{5,6},{6,7},{7,8},{8,9},{9,10},{10,1... | collective-permute-start | bytes 11912 | tf_op jit(solution)/shard_map/ppermute | solution.py:17
  14.9 0.7 copy-start.18
  981.6 80.8 %copy-start.19 = (f32[4,63]{1,0:T(4,128)S(1)}, f32[4,63]{1,0:T(4,128)}, u32[]{:S(2)}) copy-start(f32[4,63]{1,0:T(4,128)} %param.11) | copy-start | bytes 3028
  1062.4 9.4 copy-start.4
  1071.9 8.0 collective-permute-start.3
  1076.6 4.5 collective-permute-start.2
  1086.8 1.9 copy-start.9
  1086.8 1.9 copy-start.10
  1086.8 2.6 copy-start.20
  1086.8 2.8 copy-start.21
  1089.4 1.6 copy-start.11
  1089.5 1.5 copy-start.14
  1089.6 1.4 copy-start.5
  1089.7 1.3 copy-start.2
  1091.0 19.3 %all-to-all-start = ((f32[32,2,7,128]{3,1,2,0:T(2,128)}), f32[32,2,7,128]{3,1,2,0:T(2,128)S(1)}, u32[]{:S(2)}, u32[]{:S(2)}) async-start(f32[32,2,7,128]{3,1,2,0:T(2,128)} %copy.55), calls=%async_computation | async-start | bytes 458752 | tf_op jit(solution)/shard_map/all_to_all | solution.py:129
  1110.4 0.7 copy-start
  1414.6 10.4 copy-start.1
  1414.6 45.3 %copy-start.3 = (f32[32,4,128]{2,0,1:T(8,128)S(1)}, f32[32,4,128]{2,0,1:T(8,128)}, u32[]{:S(2)}) copy-start(f32[32,4,128]{2,0,1:T(8,128)} %copy-done.2) | copy-start | bytes 196612
  1414.7 45.3 %copy-start.6 = (pred[32,32]{0,1:T(8,128)(4,1)S(1)}, pred[32,32]{0,1:T(8,128)(4,1)}, u32[]{:S(2)}) copy-start(pred[32,32]{0,1:T(8,128)(4,1)} %copy-done.5) | copy-start | bytes 3076
  1414.7 45.3 %copy-start.12 = (pred[32]{0:T(512)(128)(4,1)S(1)}, pred[32]{0:T(512)(128)(4,1)}, u32[]{:S(2)}) copy-start(pred[32]{0:T(512)(128)(4,1)} %copy-done.11) | copy-start | bytes 100
  1414.7 45.3 %copy-start.15 = (pred[2,32]{1,0:T(4,128)(4,1)S(1)}, pred[2,32]{1,0:T(4,128)(4,1)}, u32[]{:S(2)}) copy-start(pred[2,32]{1,0:T(4,128)(4,1)} %copy-done.14) | copy-start | bytes 196
  1425.9 34.1 %all-to-all-start.1 = ((f32[32,2,6,128]{3,1,2,0:T(2,128)}), f32[32,2,6,128]{3,1,2,0:T(2,128)S(1)}, u32[]{:S(2)}, u32[]{:S(2)}) async-start(f32[32,2,6,128]{3,1,2,0:T(2,128)} %copy.62), calls=%async_computation.1 | async-start | bytes 393216 | tf_op jit(solution)/shard_map/all_to_all | solution.py:127
  1452.0 36.1 %copy-start.16 = (pred[2,32]{1,0:T(4,128)(4,1)}, pred[2,32]{1,0:T(4,128)(4,1)S(1)}, u32[]{:S(2)}) copy-start(pred[2,32]{1,0:T(4,128)(4,1)S(1)} %iota_compare_fusion.4) | copy-start | bytes 196
  1452.1 36.0 %copy-start.7 = (pred[32,32]{0,1:T(8,128)(4,1)}, pred[32,32]{0,1:T(8,128)(4,1)S(1)}, u32[]{:S(2)}) copy-start(pred[32,32]{0,1:T(8,128)(4,1)S(1)} %iota_compare_fusion.2) | copy-start | bytes 3076
  1461.6 26.5 %all-to-all-start.2 = ((f32[32,2,7,128]{3,1,2,0:T(2,128)}), f32[32,2,7,128]{3,1,2,0:T(2,128)S(1)}, u32[]{:S(2)}, u32[]{:S(2)}) async-start(f32[32,2,7,128]{3,1,2,0:T(2,128)} %copy.65), calls=%async_computation.2 | async-start | bytes 458752 | tf_op jit(solution)/shard_map/all_to_all | solution.py:129
  1742.9 45.4 %copy-start.8 = (pred[32,32]{0,1:T(8,128)(4,1)S(1)}, pred[32,32]{0,1:T(8,128)(4,1)}, u32[]{:S(2)}) copy-start(pred[32,32]{0,1:T(8,128)(4,1)} %copy-done.7) | copy-start | bytes 3076
  1742.9 45.4 %copy-start.13 = (pred[32]{0:T(512)(128)(4,1)S(1)}, pred[32]{0:T(512)(128)(4,1)}, u32[]{:S(2)}) copy-start(pred[32]{0:T(512)(128)(4,1)} %copy-done.11) | copy-start | bytes 100
  1742.9 45.4 %copy-start.17 = (pred[2,32]{1,0:T(4,128)(4,1)S(1)}, pred[2,32]{1,0:T(4,128)(4,1)}, u32[]{:S(2)}) copy-start(pred[2,32]{1,0:T(4,128)(4,1)} %copy-done.16) | copy-start | bytes 196
Sparse Core Ops, SparseCore 0:
  1088.8 46.7 all-gather.1
where the time goes:
time: 1800 us
  local copies, waits for them, and re-layouts  1620 us (90%)
  starting transfers between devices  55.6 us (3%)
  waiting for transfers between devices  41.7 us (2%)
  blocking collectives  34.8 us (2%)
  other arithmetic  25.6 us (1%)
    gather x4, local copies, waits for them, and re-layouts, toeplitz(): picked = jnp.take(kernel, jnp.clip(offset, 0, tap_count - 1), axis=1)  1060 us
    gather x2, local copies, waits for them, and re-layouts, lookup(): return jnp.take(flat_tile, cell_ids, axis=1).astype(jnp.float32)  507 us
    another operation x2, local copies, waits for them, and re-layouts, lookup(): flat_tile = lookup_tile.reshape(lookup_tile.shape[0], -1)  44.7 us
  transfers between devices with their start and end apart: 8, of which 5 were waited for; matrix products, arithmetic and copies ran while one was open for 60% of the time, Pallas kernels for 0%

commit v1 on v0

v1 whole, which is shorter than its diff:
```python
import functools
import jax
import jax.numpy as jnp
from jax import lax
from jax.experimental import pallas as pl
from jax.experimental.pallas import tpu as pltpu
from jax.sharding import PartitionSpec as P

MESH = pl.DeviceIdType.MESH
LENS_WEIGHTS = (0.6, 0.4)
CHANNELS = 5
EDGE = 128
WIDE = 384
F32 = jnp.float32
BF16 = jnp.bfloat16


def iota(shape, dim):
    return lax.broadcasted_iota(jnp.int32, shape, dim)


def mod(a, b):
    return lax.rem(a, b)


def split(x):
    high = x.astype(BF16)
    return high, (x - high.astype(F32)).astype(BF16)


def dot(a, b):
    return jnp.dot(a, b, preferred_element_type=F32)


def dot_t(a, b):
    return lax.dot_general(a, b, (((1,), (1,)), ((), ())), preferred_element_type=F32)


def advance(ray_state, samples, plane_weight):
    pos_x, pos_y, jac_xx, jac_xy, jac_yx, jac_yy = ray_state
    deflect_x, deflect_y, shear_one, shear_two, converge = samples
    mat_xx = converge + shear_one
    mat_yy = converge - shear_one
    return (
        pos_x - plane_weight * deflect_x,
        pos_y - plane_weight * deflect_y,
        jac_xx - plane_weight * (mat_xx * jac_xx + shear_two * jac_yx),
        jac_xy - plane_weight * (mat_xx * jac_xy + shear_two * jac_yy),
        jac_yx - plane_weight * (shear_two * jac_xx + mat_yy * jac_yx),
        jac_yy - plane_weight * (shear_two * jac_xy + mat_yy * jac_yy),
    )


def kernel(
    planes, tiles,
    kappa, row_kernel, col_kernel, positions, cells, owners, counts,
    final, jacobian,
    slab, taps, col_high, col_low, row_high, row_low, pass_high, pass_low, table,
    start_xy, cell_rows, cell_out, cell_in, stage, found, samples,
    kappa_send, kappa_recv, cell_send, cell_recv, found_send, found_recv,
):
    p, r = lax.axis_index("plane"), lax.axis_index("ray")
    k = mod(p, 2)
    base = p - k
    own_rows = kappa.shape[1]
    cols = kappa.shape[2]
    rows = planes * own_rows
    blocks = owners.shape[2]
    peers = 2 * tiles
    margin = (row_kernel.shape[1] - 1) // 2

    def peer(u):
        return mod(k + u, 2), mod(r + u // 2, tiles)

    def column_mate(e, w):
        return mod(base + 2 * e, planes) + mod(k + w, 2)

    others = [(e, w) for e in range(1, planes // 2) for w in range(2)]

    barrier = pltpu.get_barrier_semaphore()

    def greet(dp, dr):
        pl.semaphore_signal(barrier, inc=1, device_id=(dp, dr), device_id_type=MESH)

    @pl.loop(1, peers)
    def _(u):
        kk, t = peer(u)
        greet(base + kk, t)

    for e, w in others:
        dp = column_mate(e, w)
        greet(dp, r)

        @pl.when(r > 0)
        def _():
            greet(dp, r - 1)

        @pl.when(r < tiles - 1)
        def _():
            greet(dp, r + 1)

    for b in range(blocks):
        lanes = pl.ds(b * 128, 128)
        for m in range(2):
            start_xy[m, b : b + 1, :] = positions[m : m + 1, lanes]
            cell_rows[m, b : b + 1, :] = cells[m : m + 1, lanes]
    left_id = iota((blocks, blocks), 0)
    right_id = iota((blocks, blocks), 1)
    traced_row = iota((1, blocks), 1) < counts[0]
    traced_col = iota((blocks, 1), 0) < counts[0]
    target_cols = []
    for m in range(2):
        owner_row = owners[m]
        owner_col = jnp.sum(
            jnp.where(left_id == right_id, jnp.broadcast_to(owner_row, (blocks, blocks)), 0),
            axis=1, keepdims=True,
        )
        same = owner_col == owner_row
        slot_row = jnp.sum((same & (left_id < right_id)).astype(jnp.int32), axis=0, keepdims=True)
        slot_col = jnp.sum((same & (right_id < left_id)).astype(jnp.int32), axis=1, keepdims=True)
        dest_row = jnp.where(traced_row, owner_row * 2 + slot_row, -1)
        target_cols.append(jnp.where(traced_col, owner_col * 2 + slot_col, -1))
        choose = (iota((peers, blocks), 0) == dest_row).astype(F32).astype(BF16)
        ids = cell_rows[m]
        pieces = jnp.concatenate(
            [(ids >> 9).astype(F32), ((ids >> 8) & 1).astype(F32), (ids & 255).astype(F32)], axis=1
        ).astype(BF16)
        sent = dot(choose, pieces).astype(jnp.int32)
        out = sent[:, :128] * 512 + sent[:, 128:256] * 256 + sent[:, 256:]
        for t in range(tiles):
            cell_out[m, t, :, 0:128] = out[2 * t : 2 * t + 1]
            cell_out[m, t, :, 128:256] = out[2 * t + 1 : 2 * t + 2]

    sides = jnp.minimum(r, 1) + jnp.minimum(tiles - 1 - r, 1)
    pl.semaphore_wait(barrier, peers - 1 + len(others) * (1 + sides))

    def remote(src, dst, send_sem, recv_sem, dp, dr):
        return pltpu.make_async_remote_copy(
            src_ref=src, dst_ref=dst, send_sem=send_sem, recv_sem=recv_sem,
            device_id=(dp, dr), device_id_type=MESH,
        )

    order = [(e, w) for e in sorted(range(planes // 2), key=lambda e: -min(e, planes // 2 - e)) for w in (1, 0)]

    def slab_part(q, d):
        lanes = (pl.ds(EDGE, cols), pl.ds(0, EDGE), pl.ds(EDGE + cols, EDGE))[d]
        return slab.at[pl.ds(q * own_rows, own_rows), lanes]

    def kappa_part(m, d):
        lanes = (pl.ds(0, cols), pl.ds(cols - EDGE, EDGE), pl.ds(0, EDGE))[d]
        return kappa.at[m, :, lanes]

    def kappa_copy(e, w, d, sender):
        dp = column_mate(e, w)
        dr = (r, r + 1, r - 1)[d]
        return remote(
            kappa_part(mod(k + w, 2), d), slab_part(sender, d),
            kappa_send.at[e, w, d], kappa_recv.at[sender, d], dp, dr,
        )

    for e, w in order:
        if (e, w) != (0, 0):
            kappa_copy(e, w, 0, p).start()
    for e, w in order:

        @pl.when(r < tiles - 1)
        def _():
            kappa_copy(e, w, 1, p).start()

        @pl.when(r > 0)
        def _():
            kappa_copy(e, w, 2, p).start()

    def cell_copy(u):
        kk, t = peer(u)
        return remote(
            cell_out.at[kk, t], cell_in.at[k, r], cell_send.at[u], cell_recv.at[k, r], base + kk, t
        )

    def cell_arrival(u):
        kk, t = peer(u)
        return remote(
            cell_out.at[kk, t], cell_in.at[kk, t], cell_send.at[u], cell_recv.at[kk, t], base + kk, t
        )

    @pl.loop(1, peers)
    def _(u):
        cell_copy(u).start()

    cell_in[k, r] = cell_out[k, r]
    slab[pl.ds(p * own_rows, own_rows), EDGE : EDGE + cols] = kappa[k]

    @pl.when(r == 0)
    def _():
        slab[:, 0:EDGE] = jnp.zeros((rows, EDGE), BF16)

    @pl.when(r == tiles - 1)
    def _():
        slab[:, EDGE + cols :] = jnp.zeros((rows, EDGE), BF16)

    taps[...] = jnp.zeros_like(taps)
    taps[0:4, 0 : row_kernel.shape[1]] = row_kernel[...]
    taps[4:8, 0 : row_kernel.shape[1]] = col_kernel[...]
    for c in range(4):
        across = jnp.broadcast_to(taps[4 + c : 5 + c, :], (EDGE, WIDE))
        band = pltpu.roll(across, EDGE - margin, 1, stride=1, stride_axis=0)
        col_high[c * EDGE : (c + 1) * EDGE, :], col_low[c * EDGE : (c + 1) * EDGE, :] = split(band)
        down = jnp.broadcast_to(taps[c : c + 1, :], (rows, WIDE))
        band = pltpu.roll(down, WIDE - margin, 1, stride=1, stride_axis=0)[:, :rows]
        row_high[c], row_low[c] = split(band)
    stage[...] = jnp.zeros_like(stage)

    for e, w in order:
        if (e, w) != (0, 0):
            kappa_copy(e, w, 0, column_mate(e, w)).wait_recv()
    for e, w in order:

        @pl.when(r < tiles - 1)
        def _():
            kappa_copy(e, w, 2, column_mate(e, w)).wait_recv()

        @pl.when(r > 0)
        def _():
            kappa_copy(e, w, 1, column_mate(e, w)).wait_recv()

    for j in range(cols // EDGE):
        window = slab[:, j * EDGE : j * EDGE + WIDE]
        passed = dot_t(window, col_high[...]) + dot_t(window, col_low[...])
        for c in range(4):
            lanes = slice(j * EDGE, (j + 1) * EDGE)
            pass_high[c, :, lanes], pass_low[c, :, lanes] = split(passed[:, c * EDGE : (c + 1) * EDGE])
    for c in range(4):
        field = (
            dot(row_high[c], pass_high[c]) + dot(row_low[c], pass_high[c]) + dot(row_high[c], pass_low[c])
        )
        table[c * rows : (c + 1) * rows, :] = field.astype(BF16)
    table[4 * rows :, :] = slab[:, EDGE : EDGE + cols]

    @pl.loop(1, peers)
    def _(u):
        cell_arrival(u).wait_recv()

    def look_up(u):
        kk, t = peer(u)
        ids = cell_in[kk, t]
        hot = (iota((cols, 256), 0) == (ids & (cols - 1))).astype(F32).astype(BF16)
        picked = dot(table[...], hot)
        mine = iota((rows, 256), 0) == (ids >> 9)
        for c in range(CHANNELS):
            value = jnp.sum(jnp.where(mine, picked[c * rows : (c + 1) * rows], 0.0), axis=0, keepdims=True)
            stage[c : c + 1, :] = value[:, :128]
            stage[8 + c : 9 + c, :] = value[:, 128:]
        return stage[...].astype(BF16)

    def found_copy(u):
        kk, t = peer(u)
        return remote(
            found.at[u], samples.at[k, r], found_send.at[u], found_recv.at[k, r], base + kk, t
        )

    def found_arrival(u):
        kk, t = peer(u)
        return remote(
            found.at[u], samples.at[kk, t], found_send.at[u], found_recv.at[kk, t], base + kk, t
        )

    @pl.loop(1, peers)
    def _(u):
        found[u] = look_up(u)
        found_copy(u).start()

    samples[k, r] = look_up(0)

    @pl.loop(1, peers)
    def _(u):
        found_arrival(u).wait_recv()

    initial = (start_xy[0], start_xy[1], 1.0, 0.0, 0.0, 1.0)
    state = (start_xy[0], start_xy[1]) + tuple(
        jnp.full((blocks, 128), v, F32) for v in initial[2:]
    )
    for m in range(2):
        target = jnp.concatenate([target_cols[m] * 8 + c for c in range(CHANNELS)], axis=0)
        wanted = (iota((CHANNELS * blocks, tiles * 16), 1) == target).astype(F32).astype(BF16)
        got = dot(wanted, samples[m].reshape(tiles * 16, 128))
        state = advance(
            state, [got[c * blocks : (c + 1) * blocks] for c in range(CHANNELS)], LENS_WEIGHTS[m]
        )
    for v in range(6):
        value = jnp.where(traced_col, state[v], initial[v])
        ref, row = (final, v) if v < 2 else (jacobian, v - 2)
        for b in range(blocks):
            ref[row : row + 1, b * 128 : (b + 1) * 128] = value[b : b + 1]

    for e, w in order:
        if (e, w) != (0, 0):
            kappa_copy(e, w, 0, p).wait_send()
    for e, w in order:

        @pl.when(r < tiles - 1)
        def _():
            kappa_copy(e, w, 1, p).wait_send()

        @pl.when(r > 0)
        def _():
            kappa_copy(e, w, 2, p).wait_send()

    @pl.loop(1, peers)
    def _(u):
        cell_copy(u).wait_send()
        found_copy(u).wait_send()


def local(planes, tiles, kappa, row_kernel, col_kernel, positions, cells, owners, counts):
    own_rows, cols = kappa.shape[1:]
    rows = planes * own_rows
    blocks = owners.shape[1]
    rays = positions.shape[1]
    peers = 2 * tiles
    in_vmem = pl.BlockSpec(memory_space=pltpu.VMEM)
    dma = pltpu.SemaphoreType.DMA
    return pl.pallas_call(
        functools.partial(kernel, planes, tiles),
        out_shape=(
            jax.ShapeDtypeStruct((2, rays), F32),
            jax.ShapeDtypeStruct((4, rays), F32),
        ),
        in_specs=[in_vmem] * 6 + [pl.BlockSpec(memory_space=pltpu.SMEM)],
        out_specs=(in_vmem, in_vmem),
        scratch_shapes=[
            pltpu.VMEM((rows, cols + 2 * EDGE), BF16),
            pltpu.VMEM((8, WIDE), F32),
            pltpu.VMEM((4 * EDGE, WIDE), BF16),
            pltpu.VMEM((4 * EDGE, WIDE), BF16),
            pltpu.VMEM((4, rows, rows), BF16),
            pltpu.VMEM((4, rows, rows), BF16),
            pltpu.VMEM((4, rows, cols), BF16),
            pltpu.VMEM((4, rows, cols), BF16),
            pltpu.VMEM((CHANNELS * rows, cols), BF16),
            pltpu.VMEM((2, blocks, 128), F32),
            pltpu.VMEM((2, blocks, 128), jnp.int32),
            pltpu.VMEM((2, tiles, 1, 256), jnp.int32),
            pltpu.VMEM((2, tiles, 1, 256), jnp.int32),
            pltpu.VMEM((16, 128), F32),
            pltpu.VMEM((peers, 16, 128), BF16),
            pltpu.VMEM((2, tiles, 16, 128), BF16),
            dma((planes // 2, 2, 3)),
            dma((planes, 3)),
            dma((peers,)),
            dma((2, tiles)),
            dma((peers,)),
            dma((2, tiles)),
        ],
        compiler_params=pltpu.CompilerParams(
            collective_id=0, has_side_effects=True, vmem_limit_bytes=48 * 2**20
        ),
    )(kappa, row_kernel, col_kernel, positions, cells, owners.reshape(2, 1, blocks), counts)


def solution(mesh):
    return jax.shard_map(
        functools.partial(local, mesh.shape["plane"], mesh.shape["ray"]),
        mesh=mesh,
        in_specs=(
            P(None, "plane", "ray"),
            P(),
            P(),
            P(None, ("plane", "ray")),
            P(None, ("plane", "ray")),
            P(None, ("plane", "ray"), None),
            P(("plane", "ray")),
        ),
        out_specs=(P(None, ("plane", "ray")), P(None, ("plane", "ray"))),
        check_vma=False,
    )
```

time: 1800 us -> 73.3 us (0.04)
  local copies, waits for them, and re-layouts: 1620 us -> 4.95 us
  Pallas kernels: 0 us -> 66.7 us
  starting transfers between devices: 55.6 us -> 0 us
  waiting for transfers between devices: 41.7 us -> 0 us
  blocking collectives: 34.8 us -> 0 us
  other arithmetic: 25.6 us -> 0 us
    gather x6 -> x0, local copies, waits for them, and re-layouts: 1560 us -> none  [the longest x4 1060 us: toeplitz(): picked = jnp.take(kernel, jnp.clip(offset, 0, tap_count - 1), axis=1)]
    pallas_call x0 -> x1, Pallas kernels: none -> 66.7 us  [local(): pl.pallas_call(functools.partial(kernel, planes, tiles), out_shape=(jax.S...]
    another operation x6 -> x0, local copies, waits for them, and re-layouts: 45.6 us -> none  [the longest x2 44.7 us: lookup(): flat_tile = lookup_tile.reshape(lookup_tile.shape[0], -1)]
    all_to_all x3 -> x0, starting transfers between devices: 41.5 us -> none  [the longest x1 26 us: visit(): lax.all_to_all(updated, 'ray', split_axis=0, concat_axis=0, tiled=True)]
    all_to_all x1 -> x0, blocking collectives: 34.8 us -> none  [visit(): lax.all_to_all(updated, 'ray', split_axis=0, concat_axis=0, tiled=True)]
    all_gather x1 -> x0, waiting for transfers between devices: 24.5 us -> none  [local(): tile_stack = lax.all_gather(fields, 'plane', axis=2, tiled=True)]
    sub x4 -> x0, other arithmetic: 20.8 us -> none  [the longest x2 20.7 us: advance(): mat_yy = converge - shear_one]
  transfers between devices with their start and end apart: 8 -> 0, of which waited for: 5 -> 0; matrix products, arithmetic and copies ran while one was open for 60% -> 0% of each run, Pallas kernels for 0% -> 0%
where the time goes in v1:
time: 73.3 us; the launch traced here: 73 us
  Pallas kernels  66.7 us (91%)
  local copies, waits for them, and re-layouts  4.95 us (7%)
  between operations  1.32 us (2%)
    pallas_call x1, Pallas kernels, local(): pl.pallas_call(functools.partial(kernel, planes, tiles), out_shape=(jax.S...  66.7 us
    unnamed x14, local copies, waits for them, and re-layouts  4.95 us

profile of v1, /device:TPU:1, one launch (start us, length us, event | category | flops | bytes accessed | tf_op | source)
XLA Modules:
  0.0 73.0 jit_solution(15188872232176823025)
XLA Ops:
  0.6 0.0 copy-start.3
  1.3 0.0 copy-start.5
  1.3 0.0 copy-done.3
  1.3 0.7 copy-done.5
  2.0 0.0 copy-start
  2.0 0.8 %copy-done = bf16[2,32,512]{2,1,0:T(8,128)(2,1)S(1)} copy-done((bf16[2,32,512]{2,1,0:T(8,128)(2,1)S(1)}, bf16[2,32,512]{2,1,0:T(8,128)(2,1)}, u32[]{:S(2)}) %copy-start) | copy-done | bytes 65560
  2.8 0.0 copy-start.1
  2.8 0.8 %copy-done.1 = f32[2,4096]{1,0:T(2,128)S(1)} copy-done((f32[2,4096]{1,0:T(2,128)S(1)}, f32[2,4096]{1,0:T(2,128)}, u32[]{:S(2)}) %copy-start.1) | copy-done | bytes 32792
  3.6 0.0 copy-start.2
  3.6 0.8 %copy-done.2 = s32[2,4096]{1,0:T(2,128)S(1)} copy-done((s32[2,4096]{1,0:T(2,128)S(1)}, s32[2,4096]{1,0:T(2,128)}, u32[]{:S(2)}) %copy-start.2) | copy-done | bytes 32792
  4.3 0.0 copy-start.4
  4.3 0.7 copy-done.4
  5.0 66.7 %shard_map.86 = (f32[2,4096]{1,0:T(2,128)S(1)}, f32[4,4096]{1,0:T(4,128)S(1)}) custom-call(bf16[2,32,512]{2,1,0:T(8,128)(2,1)S(1)} %copy-done, f32[4,63]{1,0:T(4,128)S(1)} %copy-done.3, f32[4,63]{1,0:T(4,128)S(1)} %copy-done.4, f32[2,4096]{1,0:T(2,128)S(1)} %copy-done.1, s32[2,4096]{1,0:T(2,128)S(1)} %copy-done.2, s32[2,1,32]{2,1,0:T(1,128)S(1)} %bitcast.3, ...), custom_call_target="tpu_custom_call" | custom-call | tf_op jit(solution)/shard_map/pallas_call | solution.py:322
  71.7 0.6 copy.13
  72.3 0.6 copy.14
Async XLA Ops:
  0.6 0.7 copy-start.3
  1.3 0.7 copy-start.5
  2.0 0.8 %copy-start = (bf16[2,32,512]{2,1,0:T(8,128)(2,1)S(1)}, bf16[2,32,512]{2,1,0:T(8,128)(2,1)}, u32[]{:S(2)}) copy-start(bf16[2,32,512]{2,1,0:T(8,128)(2,1)} %kappa.1) | copy-start | bytes 196612
  2.8 0.8 %copy-start.1 = (f32[2,4096]{1,0:T(2,128)S(1)}, f32[2,4096]{1,0:T(2,128)}, u32[]{:S(2)}) copy-start(f32[2,4096]{1,0:T(2,128)} %positions.1) | copy-start | bytes 98308
  3.6 0.8 %copy-start.2 = (s32[2,4096]{1,0:T(2,128)S(1)}, s32[2,4096]{1,0:T(2,128)}, u32[]{:S(2)}) copy-start(s32[2,4096]{1,0:T(2,128)} %cells.1) | copy-start | bytes 98308
  4.3 0.7 copy-start.4

commit v2 on v1

v2 whole, which is shorter than its diff:
```python
import functools
import jax
import jax.numpy as jnp
from jax import lax
from jax.experimental import pallas as pl
from jax.experimental.pallas import tpu as pltpu
from jax.sharding import PartitionSpec as P

MESH = pl.DeviceIdType.MESH
LENS_WEIGHTS = (0.6, 0.4)
CHANNELS = 5
EDGE = 128
WIDE = 384
GROUP = 8
F32 = jnp.float32
BF16 = jnp.bfloat16


def iota(shape, dim):
    return lax.broadcasted_iota(jnp.int32, shape, dim)


def mod(a, b):
    return lax.rem(a, b)


def split(x):
    high = x.astype(BF16)
    return high, (x - high.astype(F32)).astype(BF16)


def dot(a, b):
    return jnp.dot(a, b, preferred_element_type=F32)


def dot_t(a, b):
    return lax.dot_general(a, b, (((1,), (1,)), ((), ())), preferred_element_type=F32)


def advance(ray_state, samples, plane_weight):
    pos_x, pos_y, jac_xx, jac_xy, jac_yx, jac_yy = ray_state
    deflect_x, deflect_y, shear_one, shear_two, converge = samples
    mat_xx = converge + shear_one
    mat_yy = converge - shear_one
    return (
        pos_x - plane_weight * deflect_x,
        pos_y - plane_weight * deflect_y,
        jac_xx - plane_weight * (mat_xx * jac_xx + shear_two * jac_yx),
        jac_xy - plane_weight * (mat_xx * jac_xy + shear_two * jac_yy),
        jac_yx - plane_weight * (shear_two * jac_xx + mat_yy * jac_yx),
        jac_yy - plane_weight * (shear_two * jac_xy + mat_yy * jac_yy),
    )


def kernel(
    planes, grid,
    kappa_hbm, row_kernel_hbm, col_kernel_hbm, positions_hbm, cells_hbm, owners_hbm, counts,
    final, jacobian,
    row_kernel, col_kernel, positions, cells, owners,
    slab, halo, edge, taps, col_high, col_low, row_high, row_low, pass_high, pass_low, table, rows_of,
    start_xy, cell_rows, cell_out, cell_one, cell_two, cell_in, offsets, offset_of, found, samples,
    load_sem, halo_send, halo_recv, kappa_send, kappa_recv, edge_send, edge_recv,
    cell_send, cell_recv, found_send, found_recv,
):
    tx, ty = grid
    tiles = tx * ty * 2
    p, r = lax.axis_index("plane"), lax.axis_index("ray")
    k = mod(p, 2)
    base = p - k
    x, y, zl = r // (2 * ty), mod(r // 2, ty), mod(r, 2)
    near = zl * 2 + k
    own_rows, cols = kappa_hbm.shape[1:]
    rows = planes * own_rows
    blocks = owners.shape[2]
    peers = 2 * tiles
    margin = (row_kernel.shape[1] - 1) // 2

    def peer(u):
        return mod(k + u, 2), mod(r + u // 2, tiles)

    def near_mate(w):
        q = mod(near + w, 4)
        return q, base + mod(q, 2), r - zl + q // 2

    def y_mate(w):
        yy = mod(y + w, ty)
        return yy, r + 2 * (yy - y)

    def x_mate(w):
        xx = mod(x + w, tx)
        return xx, r + 2 * ty * (xx - x)

    def column_mate(e, w):
        return mod(base + 2 * e, planes) + mod(k + w, 2)

    half = planes // 2
    order = [
        (e, w) for e in sorted(range(half), key=lambda e: -min(e, half - e)) for w in (1, 0) if (e, w) != (0, 0)
    ]
    far = [(e, w) for e, w in order if e]

    barrier = pltpu.get_barrier_semaphore()

    def greet(dp, dr):
        pl.semaphore_signal(barrier, inc=1, device_id=(dp, dr), device_id_type=MESH)

    @pl.when(r > 0)
    def _():
        greet(p, r - 1)

    @pl.when(r < tiles - 1)
    def _():
        greet(p, r + 1)

    for w in range(1, 4):
        greet(*near_mate(w)[1:])
    for e, w in far:
        greet(column_mate(e, w), r)
    for w in range(1, ty):
        greet(p, y_mate(w)[1])
    for w in range(1, tx):
        greet(p, x_mate(w)[1])

    loads = [
        pltpu.make_async_copy(src, dst, load_sem.at[i])
        for i, (src, dst) in enumerate([
            (owners_hbm, owners),
            (cells_hbm, cells),
            (row_kernel_hbm, row_kernel),
            (col_kernel_hbm, col_kernel),
            (positions_hbm, positions),
            (kappa_hbm.at[k], slab.at[pl.ds(p * own_rows, own_rows), pl.ds(EDGE, cols)]),
        ])
    ]
    for load in loads:
        load.start()
    for load in loads[:2]:
        load.wait()

    for b in range(blocks):
        lanes = pl.ds(b * 128, 128)
        for m in range(2):
            cell_rows[m, b : b + 1, :] = cells[m : m + 1, lanes]
    left_id = iota((blocks, blocks), 0)
    right_id = iota((blocks, blocks), 1)
    traced_row = iota((1, blocks), 1) < counts[0]
    traced_col = iota((blocks, 1), 0) < counts[0]
    target_cols = []
    for m in range(2):
        owner_row = owners[m]
        owner_col = jnp.sum(
            jnp.where(left_id == right_id, jnp.broadcast_to(owner_row, (blocks, blocks)), 0),
            axis=1, keepdims=True,
        )
        same = owner_col == owner_row
        slot_row = jnp.sum((same & (left_id < right_id)).astype(jnp.int32), axis=0, keepdims=True)
        slot_col = jnp.sum((same & (right_id < left_id)).astype(jnp.int32), axis=1, keepdims=True)
        dest_row = jnp.where(traced_row, owner_row * 2 + slot_row, -1)
        target_cols.append(jnp.where(traced_col, owner_col * 2 + slot_col, -1))
        choose = (iota((peers, blocks), 0) == dest_row).astype(jnp.int32)
        ids = cell_rows[m]
        out = sum(choose[:, b : b + 1] * ids[b : b + 1] for b in range(blocks))
        for t in range(tiles):
            where = (t % 2 * 2 + m, t // (2 * ty), t // 2 % ty)
            cell_out[where + (slice(None), slice(0, 128))] = out[2 * t : 2 * t + 1]
            cell_out[where + (slice(None), slice(128, 256))] = out[2 * t + 1 : 2 * t + 2]

    sides = jnp.minimum(r, 1) + jnp.minimum(tiles - 1 - r, 1)
    pl.semaphore_wait(barrier, 3 + len(far) + ty - 1 + tx - 1 + sides)

    def remote(src, dst, send_sem, recv_sem, dp, dr):
        return pltpu.make_async_remote_copy(
            src_ref=src, dst_ref=dst, send_sem=send_sem, recv_sem=recv_sem,
            device_id=(dp, dr), device_id_type=MESH,
        )

    def to_right():
        return remote(
            kappa_hbm.at[:, :, pl.ds(cols - EDGE, EDGE)], halo.at[0], halo_send.at[0], halo_recv.at[0], p, r + 1
        )

    def to_left():
        return remote(
            kappa_hbm.at[:, :, pl.ds(0, EDGE)], halo.at[1], halo_send.at[1], halo_recv.at[1], p, r - 1
        )

    def own_part(q, lanes):
        return slab.at[pl.ds(q * own_rows, own_rows), lanes]

    def kappa_copy(e, w, sender):
        return remote(
            kappa_hbm.at[mod(k + w, 2)], own_part(sender, pl.ds(EDGE, cols)),
            kappa_send.at[e, w], kappa_recv.at[sender], column_mate(e, w), r,
        )

    def edge_copy(e, w, sender):
        return remote(
            edge.at[mod(k + w, 2)], own_part(sender, pl.ds(0, EDGE)),
            edge_send.at[e, w], edge_recv.at[sender], column_mate(e, w), r,
        )

    def cell_near(w, arrival):
        q, dp, dr = near_mate(w)
        slot = q if arrival else near
        return remote(cell_out.at[q], cell_one.at[slot], cell_send.at[0, w], cell_recv.at[0, slot], dp, dr)

    def cell_y(w, arrival):
        yy, dr = y_mate(w)
        slot = yy if arrival else y
        return remote(
            cell_one.at[:, :, yy], cell_two.at[slot], cell_send.at[1, w], cell_recv.at[1, slot], p, dr
        )

    def cell_x(w, arrival):
        xx, dr = x_mate(w)
        slot = xx if arrival else x
        return remote(
            cell_two.at[:, :, xx], cell_in.at[slot], cell_send.at[2, w], cell_recv.at[2, slot], p, dr
        )

    @pl.when(r < tiles - 1)
    def _():
        to_right().start()

    @pl.when(r > 0)
    def _():
        to_left().start()

    for w in range(1, 4):
        cell_near(w, False).start()
    for e, w in order:
        kappa_copy(e, w, p).start()
    cell_one[near] = cell_out[near]

    @pl.when(r == 0)
    def _():
        halo[0] = jnp.zeros(halo.shape[1:], BF16)

    @pl.when(r == tiles - 1)
    def _():
        halo[1] = jnp.zeros(halo.shape[1:], BF16)

    for load in loads[2:]:
        load.wait()

    taps[...] = jnp.zeros_like(taps)
    taps[0:4, 0 : row_kernel.shape[1]] = row_kernel[...]
    taps[4:8, 0 : row_kernel.shape[1]] = col_kernel[...]

    def bands(c):
        across = jnp.broadcast_to(taps[4 + c : 5 + c, :], (EDGE, WIDE))
        band = pltpu.roll(across, EDGE - margin, 1, stride=1, stride_axis=0)
        col_high[c * EDGE : (c + 1) * EDGE, :], col_low[c * EDGE : (c + 1) * EDGE, :] = split(band)
        down = jnp.broadcast_to(taps[c : c + 1, :], (rows, WIDE))
        band = pltpu.roll(down, WIDE - margin, 1, stride=1, stride_axis=0)[:, :rows]
        row_high[c], row_low[c] = split(band)

    bands(0)

    @pl.when(r > 0)
    def _():
        to_right().wait_recv()

    @pl.when(r < tiles - 1)
    def _():
        to_left().wait_recv()

    for m in range(2):
        packed = jnp.where(
            iota((own_rows, EDGE), 1) < EDGE // 2, halo[1, m].astype(F32), halo[0, m].astype(F32)
        )
        edge[m] = packed.astype(BF16)
    for e, w in order:
        edge_copy(e, w, p).start()
    slab[pl.ds(p * own_rows, own_rows), 0:EDGE] = edge[k]

    for w in range(1, 4):
        cell_near(w, True).wait_recv()
    for w in range(1, ty):
        cell_y(w, False).start()
    cell_two[y] = cell_one[:, :, y]
    bands(1)
    bands(2)
    for w in range(1, ty):
        cell_y(w, True).wait_recv()
    for w in range(1, tx):
        cell_x(w, False).start()
    cell_in[x] = cell_two[:, :, x]
    bands(3)
    for b in range(blocks):
        lanes = pl.ds(b * 128, 128)
        for m in range(2):
            start_xy[m, b : b + 1, :] = positions[m : m + 1, lanes]
    for w in range(1, tx):
        cell_x(w, True).wait_recv()
    offsets[...] = cell_in[...] >> 7
    to_scalars = pltpu.make_async_copy(offsets, offset_of, load_sem.at[len(loads)])
    to_scalars.start()

    for e, w in order:
        kappa_copy(e, w, column_mate(e, w)).wait_recv()
    for e, w in order:
        edge_copy(e, w, column_mate(e, w)).wait_recv()
    slab[:, EDGE + cols :] = slab[:, 0:EDGE]

    for j in range(cols // EDGE):
        window = slab[:, j * EDGE : j * EDGE + WIDE]
        passed = dot_t(window, col_high[...]) + dot_t(window, col_low[...])
        for c in range(4):
            lanes = slice(j * EDGE, (j + 1) * EDGE)
            pass_high[c, :, lanes], pass_low[c, :, lanes] = split(passed[:, c * EDGE : (c + 1) * EDGE])
    strips = cols // 128
    flat_rows = rows_of.reshape(rows * cols // 16, 128)
    for c in range(CHANNELS):
        if c < 4:
            field = (
                dot(row_high[c], pass_high[c]) + dot(row_low[c], pass_high[c]) + dot(row_high[c], pass_low[c])
            ).astype(BF16)
        else:
            field = slab[:, EDGE : EDGE + cols]
        table[c * rows : (c + 1) * rows, :] = field
        exact = field.astype(F32)
        for j in range(strips):
            flat_rows[pl.ds(j * 8 + c, rows, stride=8 * strips), :] = exact[:, j * 128 : (j + 1) * 128]
    to_scalars.wait()

    lane = iota((8, 128), 1)
    sublane = iota((8, 128), 0)

    def place(u):
        kk, t = peer(u)
        return t // (2 * ty), mod(t // 2, ty), mod(t, 2) * 2 + kk

    def by_matmul(u):
        ids = cell_in[place(u)]
        hot = (iota((cols, 256), 0) == (ids & (cols - 1))).astype(F32).astype(BF16)
        picked = dot(table[...], hot)
        mine = iota((rows, 256), 0) == (ids >> 9)
        values = [
            jnp.sum(jnp.where(mine, picked[c * rows : (c + 1) * rows], 0.0), axis=0, keepdims=True)
            for c in range(CHANNELS)
        ]
        pad = [jnp.zeros((3, 128), F32)]
        return jnp.concatenate([v[:, :128] for v in values] + pad + [v[:, 128:] for v in values] + pad, axis=0)

    def by_rows(u):
        px, py, pq = place(u)
        slots = []
        for slot in range(2):
            low = cell_in[px, py, pq, :, slot * 128 : (slot + 1) * 128] & 127
            low = jnp.broadcast_to(low, (8, 128))
            sums = [jnp.zeros((8, 128), F32) for _ in range(4)]
            for n in range(128):
                picked = jnp.take_along_axis(rows_of[offset_of[px, py, pq, 0, slot * 128 + n]], low, axis=1)
                sums[n % 4] = jnp.where(lane == n, picked, sums[n % 4])
            total = (sums[0] + sums[1]) + (sums[2] + sums[3])
            slots.append(jnp.where(sublane < CHANNELS, total, 0.0))
        return jnp.concatenate(slots, axis=0)

    def found_copy(u, arrival):
        kk, t = peer(u)
        slot = (kk, t) if arrival else (k, r)
        return remote(
            found.at[u], samples.at[slot], found_send.at[u], found_recv.at[slot], base + kk, t
        )

    @pl.loop(0, peers // GROUP)
    def _(g):
        for i in range(GROUP):
            u = g * GROUP + i
            found[u] = (by_matmul if i < GROUP // 2 else by_rows)(u).astype(BF16)

        @pl.when(g > 0)
        def _():
            found_copy(g * GROUP, False).start()

        for i in range(1, GROUP):
            found_copy(g * GROUP + i, False).start()

    samples[k, r] = found[0]

    @pl.loop(1, peers)
    def _(u):
        found_copy(u, True).wait_recv()

    initial = (start_xy[0], start_xy[1], 1.0, 0.0, 0.0, 1.0)
    state = (start_xy[0], start_xy[1]) + tuple(
        jnp.full((blocks, 128), v, F32) for v in initial[2:]
    )
    for m in range(2):
        target = jnp.concatenate([target_cols[m] * 8 + c for c in range(CHANNELS)], axis=0)
        wanted = (iota((CHANNELS * blocks, tiles * 16), 1) == target).astype(F32).astype(BF16)
        got = dot(wanted, samples[m].reshape(tiles * 16, 128))
        state = advance(
            state, [got[c * blocks : (c + 1) * blocks] for c in range(CHANNELS)], LENS_WEIGHTS[m]
        )
    for v in range(6):
        value = jnp.where(traced_col, state[v], initial[v])
        ref, row = (final, v) if v < 2 else (jacobian, v - 2)
        for b in range(blocks):
            ref[row : row + 1, b * 128 : (b + 1) * 128] = value[b : b + 1]

    @pl.when(r < tiles - 1)
    def _():
        to_right().wait_send()

    @pl.when(r > 0)
    def _():
        to_left().wait_send()

    for e, w in order:
        kappa_copy(e, w, p).wait_send()
        edge_copy(e, w, p).wait_send()
    for w in range(1, 4):
        cell_near(w, False).wait_send()
    for w in range(1, ty):
        cell_y(w, False).wait_send()
    for w in range(1, tx):
        cell_x(w, False).wait_send()

    @pl.loop(1, peers)
    def _(u):
        found_copy(u, False).wait_send()


def local(planes, tiles, kappa, row_kernel, col_kernel, positions, cells, owners, counts):
    own_rows, cols = kappa.shape[1:]
    rows = planes * own_rows
    blocks = owners.shape[1]
    rays = positions.shape[1]
    peers = 2 * tiles
    grid = (tiles // 8, 4)
    in_vmem = pl.BlockSpec(memory_space=pltpu.VMEM)
    in_hbm = pl.BlockSpec(memory_space=pltpu.HBM)
    dma = pltpu.SemaphoreType.DMA
    vmem = pltpu.VMEM
    ints = jnp.int32
    return pl.pallas_call(
        functools.partial(kernel, planes, grid),
        out_shape=(
            jax.ShapeDtypeStruct((2, rays), F32),
            jax.ShapeDtypeStruct((4, rays), F32),
        ),
        in_specs=[in_hbm] * 6 + [pl.BlockSpec(memory_space=pltpu.SMEM)],
        out_specs=(in_vmem, in_vmem),
        scratch_shapes=[
            vmem(row_kernel.shape, F32),
            vmem(col_kernel.shape, F32),
            vmem(positions.shape, F32),
            vmem(cells.shape, ints),
            vmem((2, 1, blocks), ints),
            vmem((rows, cols + 2 * EDGE), BF16),
            vmem((2, 2, own_rows, EDGE), BF16),
            vmem((2, own_rows, EDGE), BF16),
            vmem((8, WIDE), F32),
            vmem((4 * EDGE, WIDE), BF16),
            vmem((4 * EDGE, WIDE), BF16),
            vmem((4, rows, rows), BF16),
            vmem((4, rows, rows), BF16),
            vmem((4, rows, cols), BF16),
            vmem((4, rows, cols), BF16),
            vmem((CHANNELS * rows, cols), BF16),
            vmem((rows * cols // 128, 8, 128), F32),
            vmem((2, blocks, 128), F32),
            vmem((2, blocks, 128), ints),
            vmem((4,) + grid + (1, 256), ints),
            vmem((4,) + grid + (1, 256), ints),
            vmem((grid[1], 4, grid[0], 1, 256), ints),
            vmem(grid + (4, 1, 256), ints),
            vmem(grid + (4, 1, 256), ints),
            pltpu.SMEM(grid + (4, 1, 256), ints),
            vmem((peers, 16, 128), BF16),
            vmem((2, tiles, 16, 128), BF16),
            dma((7,)),
            dma((2,)),
            dma((2,)),
            dma((planes // 2, 2)),
            dma((planes,)),
            dma((planes // 2, 2)),
            dma((planes,)),
            dma((3, 4)),
            dma((3, 4)),
            dma((peers,)),
            dma((2, tiles)),
        ],
        compiler_params=pltpu.CompilerParams(
            collective_id=0, has_side_effects=True, vmem_limit_bytes=60 * 2**20
        ),
    )(kappa, row_kernel, col_kernel, positions, cells, owners.reshape(2, 1, blocks), counts)


def solution(mesh):
    return jax.shard_map(
        functools.partial(local, mesh.shape["plane"], mesh.shape["ray"]),
        mesh=mesh,
        in_specs=(
            P(None, "plane", "ray"),
            P(),
            P(),
            P(None, ("plane", "ray")),
            P(None, ("plane", "ray")),
            P(None, ("plane", "ray"), None),
            P(("plane", "ray")),
        ),
        out_specs=(P(None, ("plane", "ray")), P(None, ("plane", "ray"))),
        check_vma=False,
    )
```

time: 73.3 us -> 54 us (0.74)
  Pallas kernels: 66.7 us -> 50.5 us
  local copies, waits for them, and re-layouts: 4.95 us -> 2.04 us
    pallas_call x1, Pallas kernels: 66.7 us -> 50.5 us  [local(): pl.pallas_call(functools.partial(kernel, planes, grid), out_shape=(jax.Sh...]
    unnamed x14 -> x4, local copies, waits for them, and re-layouts: 4.95 us -> 2.04 us
where the time goes in v2:
time: 54 us; the launch traced here: 53.8 us
  Pallas kernels  50.5 us (94%)
  local copies, waits for them, and re-layouts  2.04 us (4%)
  between operations  1.3 us (2%)
    pallas_call x1, Pallas kernels, local(): pl.pallas_call(functools.partial(kernel, planes, grid), out_shape=(jax.Sh...  50.5 us
    unnamed x4, local copies, waits for them, and re-layouts  2.04 us

profile of v2, /device:TPU:1, one launch (start us, length us, event | category | flops | bytes accessed | tf_op | source)
XLA Modules:
  0.0 53.8 jit_solution(13926602997659559028)
XLA Ops:
  1.3 50.5 %shard_map.86 = (f32[2,4096]{1,0:T(2,128)}, f32[4,4096]{1,0:T(4,128)}) custom-call(bf16[2,32,512]{2,1,0:T(8,128)(2,1)} %kappa_hbm.1, f32[4,63]{1,0:T(4,128)} %row_kernel_hbm.1, f32[4,63]{1,0:T(4,128)} %col_kernel_hbm.1, f32[2,4096]{1,0:T(2,128)} %positions_hbm.1, s32[2,4096]{1,0:T(2,128)} %cells_hbm.1, s32[2,1,32]{2,1,0:T(1,128)} %bitcast.3, s32[1]{0:T(128)S(6)} %copy.12.counts), custom_call_target="tpu_custom_call" | custom-call | tf_op jit(solution)/shard_map/pallas_call | solution.py:438
  51.8 0.0 copy-start
  51.8 1.4 %copy.13 = f32[2,4096]{1,0:T(2,128)} copy(f32[2,4096]{1,0:T(2,128)} %get-tuple-element.4) | data formatting | bytes 65536
  53.2 0.0 copy-done
  53.2 0.6 %copy.14 = f32[4,4096]{1,0:T(4,128)} copy(f32[4,4096]{1,0:T(4,128)S(1)} %copy-done) | data formatting | bytes 131072
Async XLA Ops:
  51.8 1.4 %copy-start = (f32[4,4096]{1,0:T(4,128)S(1)}, f32[4,4096]{1,0:T(4,128)}, u32[]{:S(2)}) copy-start(f32[4,4096]{1,0:T(4,128)} %get-tuple-element.5) | copy-start | bytes 196612

commit v3 on v2

--- a/solution.py
+++ b/solution.py
@@ -21,7 +21,7 @@
 
 
 def mod(a, b):
-    return lax.rem(a, b)
+    return a & (b - 1)
 
 
 def split(x):
@@ -53,21 +53,20 @@
 
 
 def kernel(
-    planes, grid,
+    planes, tiles,
     kappa_hbm, row_kernel_hbm, col_kernel_hbm, positions_hbm, cells_hbm, owners_hbm, counts,
     final, jacobian,
     row_kernel, col_kernel, positions, cells, owners,
     slab, halo, edge, taps, col_high, col_low, row_high, row_low, pass_high, pass_low, table, rows_of,
-    start_xy, cell_rows, cell_out, cell_one, cell_two, cell_in, offsets, offset_of, found, samples,
+    start_xy, cell_rows, cell_out, cell_one, cell_mid, cell_in, offsets, offset_of, found, samples,
     load_sem, halo_send, halo_recv, kappa_send, kappa_recv, edge_send, edge_recv,
-    cell_send, cell_recv, found_send, found_recv,
+    near_send, near_recv, cell_send, cell_recv, found_send, found_recv,
 ):
-    tx, ty = grid
-    tiles = tx * ty * 2
+    groups = tiles // 2
     p, r = lax.axis_index("plane"), lax.axis_index("ray")
     k = mod(p, 2)
     base = p - k
-    x, y, zl = r // (2 * ty), mod(r // 2, ty), mod(r, 2)
+    home, zl = r >> 1, mod(r, 2)
     near = zl * 2 + k
     own_rows, cols = kappa_hbm.shape[1:]
     rows = planes * own_rows
@@ -76,19 +75,15 @@
     margin = (row_kernel.shape[1] - 1) // 2
 
     def peer(u):
-        return mod(k + u, 2), mod(r + u // 2, tiles)
+        return mod(k + u, 2), mod(r + (u >> 1), tiles)
 
     def near_mate(w):
         q = mod(near + w, 4)
-        return q, base + mod(q, 2), r - zl + q // 2
-
-    def y_mate(w):
-        yy = mod(y + w, ty)
-        return yy, r + 2 * (yy - y)
-
-    def x_mate(w):
-        xx = mod(x + w, tx)
-        return xx, r + 2 * ty * (xx - x)
+        return q, base + mod(q, 2), r - zl + (q >> 1)
+
+    def group_mate(w):
+        other = mod(home + w, groups)
+        return other, r + 2 * (other - home)
 
     def column_mate(e, w):
         return mod(base + 2 * e, planes) + mod(k + w, 2)
@@ -116,10 +111,8 @@
         greet(*near_mate(w)[1:])
     for e, w in far:
         greet(column_mate(e, w), r)
-    for w in range(1, ty):
-        greet(p, y_mate(w)[1])
-    for w in range(1, tx):
-        greet(p, x_mate(w)[1])
+    for w in range(1, groups):
+        greet(p, group_mate(w)[1])
 
     loads = [
         pltpu.make_async_copy(src, dst, load_sem.at[i])
@@ -155,18 +148,18 @@
         same = owner_col == owner_row
         slot_row = jnp.sum((same & (left_id < right_id)).astype(jnp.int32), axis=0, keepdims=True)
         slot_col = jnp.sum((same & (right_id < left_id)).astype(jnp.int32), axis=1, keepdims=True)
-        dest_row = jnp.where(traced_row, owner_row * 2 + slot_row, -1)
+        dest_row = jnp.where(
+            traced_row, (owner_row & 1) * tiles + (owner_row >> 1) * 2 + slot_row, -1
+        )
         target_cols.append(jnp.where(traced_col, owner_col * 2 + slot_col, -1))
         choose = (iota((peers, blocks), 0) == dest_row).astype(jnp.int32)
         ids = cell_rows[m]
         out = sum(choose[:, b : b + 1] * ids[b : b + 1] for b in range(blocks))
-        for t in range(tiles):
-            where = (t % 2 * 2 + m, t // (2 * ty), t // 2 % ty)
-            cell_out[where + (slice(None), slice(0, 128))] = out[2 * t : 2 * t + 1]
-            cell_out[where + (slice(None), slice(128, 256))] = out[2 * t + 1 : 2 * t + 2]
+        for z in range(2):
+            cell_out[z * 2 + m] = out[z * tiles : (z + 1) * tiles]
 
     sides = jnp.minimum(r, 1) + jnp.minimum(tiles - 1 - r, 1)
-    pl.semaphore_wait(barrier, 3 + len(far) + ty - 1 + tx - 1 + sides)
+    pl.semaphore_wait(barrier, 3 + len(far) + groups - 1 + sides)
 
     def remote(src, dst, send_sem, recv_sem, dp, dr):
         return pltpu.make_async_remote_copy(
@@ -202,21 +195,17 @@
     def cell_near(w, arrival):
         q, dp, dr = near_mate(w)
         slot = q if arrival else near
-        return remote(cell_out.at[q], cell_one.at[slot], cell_send.at[0, w], cell_recv.at[0, slot], dp, dr)
-
-    def cell_y(w, arrival):
-        yy, dr = y_mate(w)
-        slot = yy if arrival else y
-        return remote(
-            cell_one.at[:, :, yy], cell_two.at[slot], cell_send.at[1, w], cell_recv.at[1, slot], p, dr
-        )
-
-    def cell_x(w, arrival):
-        xx, dr = x_mate(w)
-        slot = xx if arrival else x
-        return remote(
-            cell_two.at[:, :, xx], cell_in.at[slot], cell_send.at[2, w], cell_recv.at[2, slot], p, dr
-        )
+        return remote(cell_out.at[q], cell_one.at[slot], near_send.at[w], near_recv.at[slot], dp, dr)
+
+    def cell_far(w):
+        other, dr = group_mate(w)
+        return remote(
+            cell_mid.at[other], cell_in.at[home], cell_send.at[0], cell_recv.at[0], p, dr
+        )
+
+    def all_cells():
+        most = pl.ds(0, groups - 1)
+        return remote(cell_mid.at[most], cell_in.at[most], cell_send.at[0], cell_recv.at[0], p, r)
 
     @pl.when(r < tiles - 1)
     def _():
@@ -276,23 +265,20 @@
 
     for w in range(1, 4):
         cell_near(w, True).wait_recv()
-    for w in range(1, ty):
-        cell_y(w, False).start()
-    cell_two[y] = cell_one[:, :, y]
+    for q in range(4):
+        for g in range(groups):
+            cell_mid[g, 2 * q : 2 * q + 2, :] = cell_one[q, 2 * g : 2 * g + 2, :]
+    for w in range(1, groups):
+        cell_far(w).start()
+    cell_in[home] = cell_mid[home]
     bands(1)
     bands(2)
-    for w in range(1, ty):
-        cell_y(w, True).wait_recv()
-    for w in range(1, tx):
-        cell_x(w, False).start()
-    cell_in[x] = cell_two[:, :, x]
     bands(3)
     for b in range(blocks):
         lanes = pl.ds(b * 128, 128)
         for m in range(2):
             start_xy[m, b : b + 1, :] = positions[m : m + 1, lanes]
-    for w in range(1, tx):
-        cell_x(w, True).wait_recv()
+    all_cells().wait_recv()
     offsets[...] = cell_in[...] >> 7
     to_scalars = pltpu.make_async_copy(offsets, offset_of, load_sem.at[len(loads)])
     to_scalars.start()
@@ -327,12 +313,16 @@
     lane = iota((8, 128), 1)
     sublane = iota((8, 128), 0)
 
-    def place(u):
+    def place(u, slot):
         kk, t = peer(u)
-        return t // (2 * ty), mod(t // 2, ty), mod(t, 2) * 2 + kk
+        return t >> 1, (mod(t, 2) * 2 + kk) * 2 + slot
+
+    def ids_of(u, slot):
+        group, row = place(u, slot)
+        return cell_in[group, pl.ds(row, 1), :]
 
     def by_matmul(u):
-        ids = cell_in[place(u)]
+        ids = jnp.concatenate([ids_of(u, 0), ids_of(u, 1)], axis=1)
         hot = (iota((cols, 256), 0) == (ids & (cols - 1))).astype(F32).astype(BF16)
         picked = dot(table[...], hot)
         mine = iota((rows, 256), 0) == (ids >> 9)
@@ -344,25 +334,27 @@
         return jnp.concatenate([v[:, :128] for v in values] + pad + [v[:, 128:] for v in values] + pad, axis=0)
 
     def by_rows(u):
-        px, py, pq = place(u)
         slots = []
         for slot in range(2):
-            low = cell_in[px, py, pq, :, slot * 128 : (slot + 1) * 128] & 127
-            low = jnp.broadcast_to(low, (8, 128))
+            group, row = place(u, slot)
+            low = jnp.broadcast_to(ids_of(u, slot) & 127, (8, 128))
             sums = [jnp.zeros((8, 128), F32) for _ in range(4)]
             for n in range(128):
-                picked = jnp.take_along_axis(rows_of[offset_of[px, py, pq, 0, slot * 128 + n]], low, axis=1)
+                picked = jnp.take_along_axis(rows_of[offset_of[group, row, n]], low, axis=1)
                 sums[n % 4] = jnp.where(lane == n, picked, sums[n % 4])
             total = (sums[0] + sums[1]) + (sums[2] + sums[3])
             slots.append(jnp.where(sublane < CHANNELS, total, 0.0))
         return jnp.concatenate(slots, axis=0)
 
-    def found_copy(u, arrival):
+    def found_copy(u):
         kk, t = peer(u)
-        slot = (kk, t) if arrival else (k, r)
-        return remote(
-            found.at[u], samples.at[slot], found_send.at[u], found_recv.at[slot], base + kk, t
-        )
+        return remote(
+            found.at[u], samples.at[k * tiles + r], found_send.at[0], found_recv.at[0], base + kk, t
+        )
+
+    def all_found():
+        most = pl.ds(0, peers - 1)
+        return remote(found.at[most], samples.at[most], found_send.at[0], found_recv.at[0], p, r)
 
     @pl.loop(0, peers // GROUP)
     def _(g):
@@ -372,16 +364,13 @@
 
         @pl.when(g > 0)
         def _():
-            found_copy(g * GROUP, False).start()
+            found_copy(g * GROUP).start()
 
         for i in range(1, GROUP):
-            found_copy(g * GROUP + i, False).start()
-
-    samples[k, r] = found[0]
-
-    @pl.loop(1, peers)
-    def _(u):
-        found_copy(u, True).wait_recv()
+            found_copy(g * GROUP + i).start()
+
+    samples[k * tiles + r] = found[0]
+    all_found().wait_recv()
 
     initial = (start_xy[0], start_xy[1], 1.0, 0.0, 0.0, 1.0)
     state = (start_xy[0], start_xy[1]) + tuple(
@@ -390,7 +379,7 @@
     for m in range(2):
         target = jnp.concatenate([target_cols[m] * 8 + c for c in range(CHANNELS)], axis=0)
         wanted = (iota((CHANNELS * blocks, tiles * 16), 1) == target).astype(F32).astype(BF16)
-        got = dot(wanted, samples[m].reshape(tiles * 16, 128))
+        got = dot(wanted, samples[m * tiles : (m + 1) * tiles].reshape(tiles * 16, 128))
         state = advance(
             state, [got[c * blocks : (c + 1) * blocks] for c in range(CHANNELS)], LENS_WEIGHTS[m]
         )
@@ -413,14 +402,8 @@
         edge_copy(e, w, p).wait_send()
     for w in range(1, 4):
         cell_near(w, False).wait_send()
-    for w in range(1, ty):
-        cell_y(w, False).wait_send()
-    for w in range(1, tx):
-        cell_x(w, False).wait_send()
-
-    @pl.loop(1, peers)
-    def _(u):
-        found_copy(u, False).wait_send()
+    all_cells().wait_send()
+    all_found().wait_send()
 
 
 def local(planes, tiles, kappa, row_kernel, col_kernel, positions, cells, owners, counts):
@@ -429,14 +412,13 @@
     blocks = owners.shape[1]
     rays = positions.shape[1]
     peers = 2 * tiles
-    grid = (tiles // 8, 4)
     in_vmem = pl.BlockSpec(memory_space=pltpu.VMEM)
     in_hbm = pl.BlockSpec(memory_space=pltpu.HBM)
     dma = pltpu.SemaphoreType.DMA
     vmem = pltpu.VMEM
     ints = jnp.int32
     return pl.pallas_call(
-        functools.partial(kernel, planes, grid),
+        functools.partial(kernel, planes, tiles),
         out_shape=(
             jax.ShapeDtypeStruct((2, rays), F32),
             jax.ShapeDtypeStruct((4, rays), F32),
@@ -463,14 +445,14 @@
             vmem((rows * cols // 128, 8, 128), F32),
             vmem((2, blocks, 128), F32),
             vmem((2, blocks, 128), ints),
-            vmem((4,) + grid + (1, 256), ints),
-            vmem((4,) + grid + (1, 256), ints),
-            vmem((grid[1], 4, grid[0], 1, 256), ints),
-            vmem(grid + (4, 1, 256), ints),
-            vmem(grid + (4, 1, 256), ints),
-            pltpu.SMEM(grid + (4, 1, 256), ints),
+            vmem((4, tiles, 128), ints),
+            vmem((4, tiles, 128), ints),
+            vmem((tiles // 2, 8, 128), ints),
+            vmem((tiles // 2, 8, 128), ints),
+            vmem((tiles // 2, 8, 128), ints),
+            pltpu.SMEM((tiles // 2, 8, 128), ints),
             vmem((peers, 16, 128), BF16),
-            vmem((2, tiles, 16, 128), BF16),
+            vmem((peers, 16, 128), BF16),
             dma((7,)),
             dma((2,)),
             dma((2,)),
@@ -478,10 +460,12 @@
             dma((planes,)),
             dma((planes // 2, 2)),
             dma((planes,)),
-            dma((3, 4)),
-            dma((3, 4)),
-            dma((peers,)),
-            dma((2, tiles)),
+            dma((4,)),
+            dma((4,)),
+            dma((1,)),
+            dma((1,)),
+            dma((1,)),
+            dma((1,)),
         ],
         compiler_params=pltpu.CompilerParams(
             collective_id=0, has_side_effects=True, vmem_limit_bytes=60 * 2**20

time: 54 us -> 49.6 us (0.919)
  Pallas kernels: 50.5 us -> 46.1 us
    pallas_call x1, Pallas kernels: 50.5 us -> 46.1 us  [local(): pl.pallas_call(functools.partial(kernel, planes, tiles), out_shape=(jax.S...]
where the time goes in v3:
time: 49.6 us; the launch traced here: 49.4 us
  Pallas kernels  46.1 us (93%)
  local copies, waits for them, and re-layouts  2.04 us (4%)
  between operations  1.3 us (3%)
    pallas_call x1, Pallas kernels, local(): pl.pallas_call(functools.partial(kernel, planes, tiles), out_shape=(jax.S...  46.1 us
    unnamed x4, local copies, waits for them, and re-layouts  2.04 us

profile of v3, /device:TPU:1, one launch (start us, length us, event | category | flops | bytes accessed | tf_op | source)
XLA Modules:
  0.0 49.4 jit_solution(4531819607328124493)
XLA Ops:
  1.3 46.1 %shard_map.86 = (f32[2,4096]{1,0:T(2,128)}, f32[4,4096]{1,0:T(4,128)}) custom-call(bf16[2,32,512]{2,1,0:T(8,128)(2,1)} %kappa_hbm.1, f32[4,63]{1,0:T(4,128)} %row_kernel_hbm.1, f32[4,63]{1,0:T(4,128)} %col_kernel_hbm.1, f32[2,4096]{1,0:T(2,128)} %positions_hbm.1, s32[2,4096]{1,0:T(2,128)} %cells_hbm.1, s32[2,1,32]{2,1,0:T(1,128)} %bitcast.3, s32[1]{0:T(128)S(6)} %copy.12.counts), custom_call_target="tpu_custom_call" | custom-call | tf_op jit(solution)/shard_map/pallas_call | solution.py:420
  47.3 0.0 copy-start
  47.4 1.4 %copy.13 = f32[2,4096]{1,0:T(2,128)} copy(f32[2,4096]{1,0:T(2,128)} %get-tuple-element.4) | data formatting | bytes 65536
  48.8 0.0 copy-done
  48.8 0.6 %copy.14 = f32[4,4096]{1,0:T(4,128)} copy(f32[4,4096]{1,0:T(4,128)S(1)} %copy-done) | data formatting | bytes 131072
Async XLA Ops:
  47.3 1.4 %copy-start = (f32[4,4096]{1,0:T(4,128)S(1)}, f32[4,4096]{1,0:T(4,128)}, u32[]{:S(2)}) copy-start(f32[4,4096]{1,0:T(4,128)} %get-tuple-element.5) | copy-start | bytes 196612

commit v4 on v3

--- a/solution.py
+++ b/solution.py
@@ -54,9 +54,9 @@
 
 def kernel(
     planes, tiles,
-    kappa_hbm, row_kernel_hbm, col_kernel_hbm, positions_hbm, cells_hbm, owners_hbm, counts,
+    kappa_hbm, row_kernel_hbm, col_kernel_hbm, positions_hbm, cells_hbm, owners_hbm, counts_hbm,
     final, jacobian,
-    row_kernel, col_kernel, positions, cells, owners,
+    row_kernel, col_kernel, positions, cells, owners, counts,
     slab, halo, edge, taps, col_high, col_low, row_high, row_low, pass_high, pass_low, table, rows_of,
     start_xy, cell_rows, cell_out, cell_one, cell_mid, cell_in, offsets, offset_of, found, samples,
     load_sem, halo_send, halo_recv, kappa_send, kappa_recv, edge_send, edge_recv,
@@ -94,6 +94,21 @@
     ]
     far = [(e, w) for e, w in order if e]
 
+    loads = [
+        pltpu.make_async_copy(src, dst, load_sem.at[i])
+        for i, (src, dst) in enumerate([
+            (owners_hbm, owners),
+            (cells_hbm, cells),
+            (counts_hbm, counts),
+            (row_kernel_hbm, row_kernel),
+            (col_kernel_hbm, col_kernel),
+            (positions_hbm, positions),
+            (kappa_hbm.at[k], slab.at[pl.ds(p * own_rows, own_rows), pl.ds(EDGE, cols)]),
+        ])
+    ]
+    for load in loads[:3]:
+        load.start()
+
     barrier = pltpu.get_barrier_semaphore()
 
     def greet(dp, dr):
@@ -114,20 +129,7 @@
     for w in range(1, groups):
         greet(p, group_mate(w)[1])
 
-    loads = [
-        pltpu.make_async_copy(src, dst, load_sem.at[i])
-        for i, (src, dst) in enumerate([
-            (owners_hbm, owners),
-            (cells_hbm, cells),
-            (row_kernel_hbm, row_kernel),
-            (col_kernel_hbm, col_kernel),
-            (positions_hbm, positions),
-            (kappa_hbm.at[k], slab.at[pl.ds(p * own_rows, own_rows), pl.ds(EDGE, cols)]),
-        ])
-    ]
-    for load in loads:
-        load.start()
-    for load in loads[:2]:
+    for load in loads[:3]:
         load.wait()
 
     for b in range(blocks):
@@ -219,6 +221,8 @@
         cell_near(w, False).start()
     for e, w in order:
         kappa_copy(e, w, p).start()
+    for load in loads[3:]:
+        load.start()
     cell_one[near] = cell_out[near]
 
     @pl.when(r == 0)
@@ -229,7 +233,7 @@
     def _():
         halo[1] = jnp.zeros(halo.shape[1:], BF16)
 
-    for load in loads[2:]:
+    for load in loads[3:]:
         load.wait()
 
     taps[...] = jnp.zeros_like(taps)
@@ -285,16 +289,22 @@
 
     for e, w in order:
         kappa_copy(e, w, column_mate(e, w)).wait_recv()
-    for e, w in order:
-        edge_copy(e, w, column_mate(e, w)).wait_recv()
-    slab[:, EDGE + cols :] = slab[:, 0:EDGE]
-
-    for j in range(cols // EDGE):
+
+    def strip(j):
         window = slab[:, j * EDGE : j * EDGE + WIDE]
         passed = dot_t(window, col_high[...]) + dot_t(window, col_low[...])
         for c in range(4):
             lanes = slice(j * EDGE, (j + 1) * EDGE)
             pass_high[c, :, lanes], pass_low[c, :, lanes] = split(passed[:, c * EDGE : (c + 1) * EDGE])
+
+    last = cols // EDGE - 1
+    for j in range(1, last):
+        strip(j)
+    for e, w in order:
+        edge_copy(e, w, column_mate(e, w)).wait_recv()
+    slab[:, EDGE + cols :] = slab[:, 0:EDGE]
+    strip(0)
+    strip(last)
     strips = cols // 128
     flat_rows = rows_of.reshape(rows * cols // 16, 128)
     for c in range(CHANNELS):
@@ -423,7 +433,7 @@
             jax.ShapeDtypeStruct((2, rays), F32),
             jax.ShapeDtypeStruct((4, rays), F32),
         ),
-        in_specs=[in_hbm] * 6 + [pl.BlockSpec(memory_space=pltpu.SMEM)],
+        in_specs=[in_hbm] * 7,
         out_specs=(in_vmem, in_vmem),
         scratch_shapes=[
             vmem(row_kernel.shape, F32),
@@ -431,6 +441,7 @@
             vmem(positions.shape, F32),
             vmem(cells.shape, ints),
             vmem((2, 1, blocks), ints),
+            pltpu.SMEM(counts.shape, ints),
             vmem((rows, cols + 2 * EDGE), BF16),
             vmem((2, 2, own_rows, EDGE), BF16),
             vmem((2, own_rows, EDGE), BF16),
@@ -453,7 +464,7 @@
             pltpu.SMEM((tiles // 2, 8, 128), ints),
             vmem((peers, 16, 128), BF16),
             vmem((peers, 16, 128), BF16),
-            dma((7,)),
+            dma((8,)),
             dma((2,)),
             dma((2,)),
             dma((planes // 2, 2)),

time: 49.6 us -> 49.4 us (level)
  no operation moved by 1% of the time
where the time goes in v4:
time: 49.4 us; the launch traced here: 49.1 us
  Pallas kernels  45.8 us (93%)
  local copies, waits for them, and re-layouts  2.04 us (4%)
  between operations  1.3 us (3%)
    pallas_call x1, Pallas kernels, local(): pl.pallas_call(functools.partial(kernel, planes, tiles), out_shape=(jax.S...  45.8 us
    unnamed x4, local copies, waits for them, and re-layouts  2.04 us

profile of v4, /device:TPU:1, one launch (start us, length us, event | category | flops | bytes accessed | tf_op | source)
XLA Modules:
  0.0 49.1 jit_solution(10390632794685589347)
XLA Ops:
  1.3 45.8 %shard_map.86 = (f32[2,4096]{1,0:T(2,128)}, f32[4,4096]{1,0:T(4,128)}) custom-call(bf16[2,32,512]{2,1,0:T(8,128)(2,1)} %kappa_hbm.1, f32[4,63]{1,0:T(4,128)} %row_kernel_hbm.1, f32[4,63]{1,0:T(4,128)} %col_kernel_hbm.1, f32[2,4096]{1,0:T(2,128)} %positions_hbm.1, s32[2,4096]{1,0:T(2,128)} %cells_hbm.1, s32[2,1,32]{2,1,0:T(1,128)} %bitcast.3, ...), custom_call_target="tpu_custom_call" | custom-call | tf_op jit(solution)/shard_map/pallas_call | solution.py:430
  47.1 0.0 copy-start
  47.1 1.4 %copy.13 = f32[2,4096]{1,0:T(2,128)} copy(f32[2,4096]{1,0:T(2,128)} %get-tuple-element.4) | data formatting | bytes 65536
  48.5 0.0 copy-done
  48.5 0.6 %copy.14 = f32[4,4096]{1,0:T(4,128)} copy(f32[4,4096]{1,0:T(4,128)S(1)} %copy-done) | data formatting | bytes 131072
Async XLA Ops:
  47.1 1.4 %copy-start = (f32[4,4096]{1,0:T(4,128)S(1)}, f32[4,4096]{1,0:T(4,128)}, u32[]{:S(2)}) copy-start(f32[4,4096]{1,0:T(4,128)} %get-tuple-element.5) | copy-start | bytes 196612

commit v5 on v4

--- a/solution.py
+++ b/solution.py
@@ -11,7 +11,8 @@
 CHANNELS = 5
 EDGE = 128
 WIDE = 384
-GROUP = 8
+GROUP = 16
+BY_MATMUL = 7
 F32 = jnp.float32
 BF16 = jnp.bfloat16
 
@@ -370,7 +371,7 @@
     def _(g):
         for i in range(GROUP):
             u = g * GROUP + i
-            found[u] = (by_matmul if i < GROUP // 2 else by_rows)(u).astype(BF16)
+            found[u] = (by_matmul if i < BY_MATMUL else by_rows)(u).astype(BF16)
 
         @pl.when(g > 0)
         def _():

time: 49.4 us -> 48.3 us (0.978)
  Pallas kernels: 45.8 us -> 44.6 us
    pallas_call x1, Pallas kernels: 45.8 us -> 44.6 us  [local(): pl.pallas_call(functools.partial(kernel, planes, tiles), out_shape=(jax.S...]
where the time goes in v5:
time: 48.3 us; the launch traced here: 48 us
  Pallas kernels  44.6 us (92%)
  local copies, waits for them, and re-layouts  2.04 us (4%)
  between operations  1.3 us (3%)
    pallas_call x1, Pallas kernels, local(): pl.pallas_call(functools.partial(kernel, planes, tiles), out_shape=(jax.S...  44.6 us
    unnamed x4, local copies, waits for them, and re-layouts  2.04 us

profile of v5, /device:TPU:1, one launch (start us, length us, event | category | flops | bytes accessed | tf_op | source)
XLA Modules:
  0.0 48.0 jit_solution(12925737778009901398)
XLA Ops:
  1.3 44.6 %shard_map.86 = (f32[2,4096]{1,0:T(2,128)}, f32[4,4096]{1,0:T(4,128)}) custom-call(bf16[2,32,512]{2,1,0:T(8,128)(2,1)} %kappa_hbm.1, f32[4,63]{1,0:T(4,128)} %row_kernel_hbm.1, f32[4,63]{1,0:T(4,128)} %col_kernel_hbm.1, f32[2,4096]{1,0:T(2,128)} %positions_hbm.1, s32[2,4096]{1,0:T(2,128)} %cells_hbm.1, s32[2,1,32]{2,1,0:T(1,128)} %bitcast.3, ...), custom_call_target="tpu_custom_call" | custom-call | tf_op jit(solution)/shard_map/pallas_call | solution.py:431
  45.9 0.0 copy-start
  45.9 1.4 %copy.13 = f32[2,4096]{1,0:T(2,128)} copy(f32[2,4096]{1,0:T(2,128)} %get-tuple-element.4) | data formatting | bytes 65536
  47.3 0.0 copy-done
  47.3 0.6 %copy.14 = f32[4,4096]{1,0:T(4,128)} copy(f32[4,4096]{1,0:T(4,128)S(1)} %copy-done) | data formatting | bytes 131072
Async XLA Ops:
  45.9 1.4 %copy-start = (f32[4,4096]{1,0:T(4,128)S(1)}, f32[4,4096]{1,0:T(4,128)}, u32[]{:S(2)}) copy-start(f32[4,4096]{1,0:T(4,128)} %get-tuple-element.5) | copy-start | bytes 196612

commit v6 on v5

--- a/solution.py
+++ b/solution.py
@@ -371,7 +371,7 @@
     def _(g):
         for i in range(GROUP):
             u = g * GROUP + i
-            found[u] = (by_matmul if i < BY_MATMUL else by_rows)(u).astype(BF16)
+            found[u] = (by_matmul if i % 2 and i < 2 * BY_MATMUL else by_rows)(u).astype(BF16)
 
         @pl.when(g > 0)
         def _():
@@ -381,6 +381,20 @@
             found_copy(g * GROUP + i).start()
 
     samples[k * tiles + r] = found[0]
+    @pl.when(r < tiles - 1)
+    def _():
+        to_right().wait_send()
+
+    @pl.when(r > 0)
+    def _():
+        to_left().wait_send()
+
+    for e, w in order:
+        kappa_copy(e, w, p).wait_send()
+        edge_copy(e, w, p).wait_send()
+    for w in range(1, 4):
+        cell_near(w, False).wait_send()
+    all_cells().wait_send()
     all_found().wait_recv()
 
     initial = (start_xy[0], start_xy[1], 1.0, 0.0, 0.0, 1.0)
@@ -400,20 +414,6 @@
         for b in range(blocks):
             ref[row : row + 1, b * 128 : (b + 1) * 128] = value[b : b + 1]
 
-    @pl.when(r < tiles - 1)
-    def _():
-        to_right().wait_send()
-
-    @pl.when(r > 0)
-    def _():
-        to_left().wait_send()
-
-    for e, w in order:
-        kappa_copy(e, w, p).wait_send()
-        edge_copy(e, w, p).wait_send()
-    for w in range(1, 4):
-        cell_near(w, False).wait_send()
-    all_cells().wait_send()
     all_found().wait_send()
 
 

time: 48.3 us -> 48.3 us (level)
  no operation moved by 1% of the time
where the time goes in v6:
time: 48.3 us; the launch traced here: 47.9 us
  Pallas kernels  44.5 us (92%)
  local copies, waits for them, and re-layouts  2.04 us (4%)
  between operations  1.3 us (3%)
    pallas_call x1, Pallas kernels, local(): pl.pallas_call(functools.partial(kernel, planes, tiles), out_shape=(jax.S...  44.5 us
    unnamed x4, local copies, waits for them, and re-layouts  2.04 us

profile of v6, /device:TPU:1, one launch (start us, length us, event | category | flops | bytes accessed | tf_op | source)
XLA Modules:
  0.0 47.9 jit_solution(9157243787662295570)
XLA Ops:
  1.3 44.5 %shard_map.86 = (f32[2,4096]{1,0:T(2,128)}, f32[4,4096]{1,0:T(4,128)}) custom-call(bf16[2,32,512]{2,1,0:T(8,128)(2,1)} %kappa_hbm.1, f32[4,63]{1,0:T(4,128)} %row_kernel_hbm.1, f32[4,63]{1,0:T(4,128)} %col_kernel_hbm.1, f32[2,4096]{1,0:T(2,128)} %positions_hbm.1, s32[2,4096]{1,0:T(2,128)} %cells_hbm.1, s32[2,1,32]{2,1,0:T(1,128)} %bitcast.3, ...), custom_call_target="tpu_custom_call" | custom-call | tf_op jit(solution)/shard_map/pallas_call | solution.py:431
  45.8 0.0 copy-start
  45.8 1.4 %copy.13 = f32[2,4096]{1,0:T(2,128)} copy(f32[2,4096]{1,0:T(2,128)} %get-tuple-element.4) | data formatting | bytes 65536
  47.2 0.0 copy-done
  47.2 0.6 %copy.14 = f32[4,4096]{1,0:T(4,128)} copy(f32[4,4096]{1,0:T(4,128)S(1)} %copy-done) | data formatting | bytes 131072
Async XLA Ops:
  45.8 1.4 %copy-start = (f32[4,4096]{1,0:T(4,128)S(1)}, f32[4,4096]{1,0:T(4,128)}, u32[]{:S(2)}) copy-start(f32[4,4096]{1,0:T(4,128)} %get-tuple-element.5) | copy-start | bytes 196612
